TPU v7x, 256 devices: a whole 4x4x8 slice. The times are simulated.
256 devices in a mesh: ctx: 32 (over y, z_lo, x), tp: 8 (over z_hi, core).
Axes of the slice: x: 4, y: 4, z: 8 (z_hi: 4, z_lo: 2; z = z_hi * 2 + z_lo), core: 2. Of those that a mesh axis runs over, the one named last changes fastest.
Arguments:
- tokens: bfloat16 [8192, 4096], P('ctx', 'tp'), may hold values from -6 to 6
- norm_gain: bfloat16 [4096], replicated, may hold values from 0.5 to 1.5
- w_query: bfloat16 [4096, 4096], P(None, 'tp'), may hold values from -2 to 2
- w_key: bfloat16 [4096, 1024], P(None, 'tp'), may hold values from -6 to 6
- w_value: bfloat16 [4096, 1024], P(None, 'tp'), may hold values from -0.09375 to 0.09375
- w_output: bfloat16 [4096, 4096], P('tp'), may hold values from -0.375 to 0.375
Outputs:
- update: bfloat16 [8192, 4096], P('ctx', 'tp')
All inputs are finite; a program needn't handle non-finite values.
Results may differ from a plain program's by a relative error of at most 0.02.
The roundings to bfloat16 on the way count: a program that leaves them out, or rounds other values in their place, can miss the bound.
Values may be sent and summed in bfloat16 or wider, within the bound.
A program may use at most 64 MiB of HBM per device.

v0:
```python
import math

import jax
import jax.numpy as jnp
from jax import lax
from jax.sharding import PartitionSpec as P

HEAD_DIM = 128


def rotate(field, positions):
    half_dim = field.shape[-1] // 2
    frequency = 500000.0 ** (-2.0 * jnp.arange(half_dim, dtype=jnp.float32) / (2 * half_dim))
    angles = positions.astype(jnp.float32)[:, None] * frequency[None, :]
    cosine = jnp.cos(angles)
    sine = jnp.sin(angles)
    first = field[..., :half_dim]
    second = field[..., half_dim:]
    return jnp.concatenate(
        [first * cosine - second * sine, second * cosine + first * sine], axis=-1
    )


def fold_keys(partial_state, shard_rows, queries, query_pos, group_rows):
    key_count = shard_rows.shape[2]
    block_rows = math.gcd(key_count, 1024)
    block_count = key_count // block_rows
    score_scale = 1.0 / queries.shape[-1] ** 0.5
    all_rows = queries.shape[1]
    group_count = all_rows // group_rows
    group_top = jnp.max(query_pos.reshape(group_count, group_rows), axis=1)

    def advance(block_index, running):
        offset = block_index * block_rows
        key_block = lax.dynamic_slice_in_dim(shard_rows[0], offset, block_rows, 1)
        value_block = lax.dynamic_slice_in_dim(shard_rows[1], offset, block_rows, 1)
        key_pos = offset + jnp.arange(block_rows, dtype=jnp.int32)
        start_group = jnp.sum((group_top < offset).astype(jnp.int32))

        def per_group(group_index, current):
            row_all, denom_all, accum_all = current
            row_start = group_index * group_rows
            group_query = lax.dynamic_slice_in_dim(queries, row_start, group_rows, 1)
            group_pos = lax.dynamic_slice_in_dim(query_pos, row_start, group_rows, 0)
            row_max = lax.dynamic_slice_in_dim(row_all, row_start, group_rows, 1)
            denominator = lax.dynamic_slice_in_dim(denom_all, row_start, group_rows, 1)
            accumulated = lax.dynamic_slice_in_dim(accum_all, row_start, group_rows, 1)
            scores = (
                jnp.einsum(
                    "brk,bnk->brn", group_query, key_block, preferred_element_type=jnp.float32
                )
                * score_scale
            )
            allowed = key_pos[None, None, :] <= group_pos[None, :, None]
            scores = jnp.where(allowed, scores, -1e30)
            newest = jnp.maximum(row_max, jnp.max(scores, axis=-1))
            weights = jnp.where(allowed, jnp.exp(scores - newest[..., None]), 0.0)
            factor = jnp.exp(row_max - newest)
            denominator = denominator * factor + jnp.sum(weights, axis=-1)
            accumulated = accumulated * factor[..., None] + jnp.einsum(
                "brn,bnk->brk",
                weights.astype(jnp.bfloat16),
                value_block,
                preferred_element_type=jnp.float32,
            )
            return (
                lax.dynamic_update_slice_in_dim(row_all, newest, row_start, 1),
                lax.dynamic_update_slice_in_dim(denom_all, denominator, row_start, 1),
                lax.dynamic_update_slice_in_dim(accum_all, accumulated, row_start, 1),
            )

        return lax.fori_loop(start_group, group_count, per_group, running)

    return lax.fori_loop(0, block_count, advance, partial_state)


def empty_state(queries):
    batch_heads, query_rows, head_size = queries.shape
    return (
        jnp.full((batch_heads, query_rows), -1e30, jnp.float32),
        jnp.zeros((batch_heads, query_rows), jnp.float32),
        jnp.zeros((batch_heads, query_rows, head_size), jnp.float32),
    )


def finish(final_state):
    return (final_state[2] / final_state[1][..., None]).astype(jnp.bfloat16)


def body(tokens, norm_gain, w_query, w_key, w_value, w_output):
    gathered = lax.all_gather(tokens, "tp", axis=1, tiled=True)
    widened = gathered.astype(jnp.float32)
    normed = (
        widened
        * lax.rsqrt(jnp.mean(widened * widened, axis=-1, keepdims=True) + 1e-05)
        * norm_gain.astype(jnp.float32)
    ).astype(jnp.bfloat16)
    tok_rows = gathered.shape[0]
    model_width = gathered.shape[1]
    head_size = HEAD_DIM
    heads_local = w_query.shape[1] // head_size
    kv_local = w_key.shape[1] // head_size
    ctx_index = lax.axis_index("ctx")
    local_pos = ctx_index * tok_rows + jnp.arange(tok_rows, dtype=jnp.int32)
    query = jnp.einsum(
        "td,dhk->htk",
        normed,
        w_query.reshape(model_width, heads_local, head_size),
        preferred_element_type=jnp.float32,
    )
    query = rotate(query, local_pos).astype(jnp.bfloat16)
    key_rows = jnp.einsum(
        "td,dhk->htk",
        normed,
        w_key.reshape(model_width, kv_local, head_size),
        preferred_element_type=jnp.float32,
    )
    key_rows = rotate(key_rows, local_pos).astype(jnp.bfloat16)
    value_rows = jnp.einsum(
        "td,dhk->htk",
        normed,
        w_value.reshape(model_width, kv_local, head_size),
        preferred_element_type=jnp.float32,
    ).astype(jnp.bfloat16)
    kv_stack = jnp.stack([key_rows, value_rows])
    ctx_count = lax.axis_size("ctx")
    sub_count = ctx_count // heads_local
    sub_rows = tok_rows // sub_count
    arrived = lax.all_to_all(
        query.reshape(heads_local * sub_count, sub_rows, head_size),
        "ctx",
        split_axis=0,
        concat_axis=0,
        tiled=True,
    )
    queries = arrived.reshape(1, ctx_count * sub_rows, head_size)
    sub_slot = ctx_index % sub_count
    query_pos = (
        jnp.arange(ctx_count, dtype=jnp.int32)[:, None] * tok_rows
        + sub_slot * sub_rows
        + jnp.arange(sub_rows, dtype=jnp.int32)[None, :]
    ).reshape(-1)
    row_group = math.gcd(ctx_count * sub_rows, 256)
    final_state = fold_keys(
        empty_state(queries),
        lax.all_gather(kv_stack, "ctx", axis=2, tiled=True),
        queries,
        query_pos,
        row_group,
    )
    result = finish(final_state).reshape(ctx_count, sub_rows, head_size)
    returned = lax.all_to_all(result, "ctx", split_axis=0, concat_axis=0, tiled=True)
    attention = returned.reshape(heads_local, tok_rows, head_size)
    group_term = jnp.einsum(
        "htk,hkd->td",
        attention,
        w_output.reshape(heads_local, head_size, model_width),
        preferred_element_type=jnp.float32,
    )
    summed = lax.psum_scatter(
        group_term.astype(jnp.bfloat16), "tp", scatter_dimension=1, tiled=True
    )
    return summed


def solution(mesh):
    placed = (P("ctx", "tp"), P(), P(None, "tp"), P(None, "tp"), P(None, "tp"), P("tp", None))
    return jax.shard_map(
        body, mesh=mesh, in_specs=placed, out_specs=P("ctx", "tp"), check_vma=False
    )
```

profile of v0, /device:TPU:1, one launch (start us, length us, event | category | flops | bytes accessed | tf_op | source)
XLA Modules:
  0.0 373.4 jit_solution(16153267084621779823)
XLA Ops:
  8.0 41.9 %all-gather.3.cloned.1.call-done = bf16[256,4096]{1,0:T(8,128)(2,1)} async-done(((bf16[256,512]{1,0:T(8,128)(2,1)}), bf16[256,4096]{1,0:T(8,128)(2,1)}) %all-gather.3.cloned.1.call-update) | async-done | bytes 2097168 | tf_op jit(solution)/shard_map/all_gather | solution.py:91
  52.2 2.5 convolution_bitcast_fusion.2
  57.1 4.1 %fusion.39 = f32[256,512]{0,1:S(1)} fusion(bf16[4096,512]{1,0:T(8,128)(2,1)} %param.12, bf16[256,4096]{1,0:T(8,128)(2,1)S(1)} %copy-done.1, f32[4096]{0:T(1024)S(1)} %convert_element_type.59, f32[256]{0:T(256)S(1)} %add_rsqrt_fusion), kind=kOutput, calls=%fused_computation.69 | convolution fusion | flops 1077936128 | bytes 6833152
  62.5 6.8 %all-to-all-start = ((bf16[32,32,128]{2,1,0:T(8,128)(2,1)}), bf16[32,32,128]{2,1,0:T(8,128)(2,1)S(1)}, u32[]{:S(2)}, u32[]{:S(2)}) async-start(bf16[32,32,128]{2,1,0:T(8,128)(2,1)} %pad_maximum_fusion), calls=%async_computation | async-start | bytes 524288 | tf_op jit(solution)/shard_map/all_to_all | solution.py:129
  69.6 107.2 %all-gather.5.cloned.1.call-done = bf16[2,1,8192,128]{2,3,1,0:T(8,128)(2,1)} async-done(((bf16[2,1,256,128]{2,3,1,0:T(8,128)(2,1)}), bf16[2,1,8192,128]{2,3,1,0:T(8,128)(2,1)}) %all-gather.5.cloned.1.call-update) | async-done | bytes 4194320 | tf_op jit(solution)/shard_map/all_gather | solution.py:146
  176.9 6.3 %copy.19 = bf16[2,1,8192,128]{3,2,1,0:T(8,128)(2,1)} copy(bf16[2,1,8192,128]{2,3,1,0:T(8,128)(2,1)} %all-gather.5.cloned.1.call-done) | data formatting | bytes 8388608
  183.3 105.4 %while.49 = (s32[]{:T(128)}, f32[1,1024]{1,0:T(1,128)S(1)}, f32[1,1024]{1,0:T(1,128)S(1)}, f32[1,1024,128]{2,1,0:T(8,128)S(1)}, s32[4]{0:T(128)S(1)}, /*index=5*...) while((s32[]{:T(128)}, f32[1,1024]{1,0:T(1,128)S(1)}, ...), condition=%wide.region_8.9_spmd.clone, body=%wide.region_2.8_spmd.clone.sunk | while | flops 137431568 | bytes 13501066 | solution.py:74
  183.3 2.5 fusion.59
  186.7 15.3 %while.50 = (s32[]{:T(128)}, f32[1,1024]{1,0:T(1,128)S(1)}, f32[1,1024]{1,0:T(1,128)S(1)}, f32[1,1024,128]{2,1,0:T(8,128)S(1)}, s32[1024]{0:T(1024)S(1)}, /*inde...) while((s32[]{:T(128)}, f32[1,1024]{1,0:T(1,128)S(1)}, ...), condition=%wide.region_7.7_spmd.clone, body=%wide.region_4.6_spmd.clone.sunk | while | flops 137430528 | bytes 4051139 | solution.py:72
  202.0 2.5 fusion.59
  205.3 15.3 %while.50 = (s32[]{:T(128)}, f32[1,1024]{1,0:T(1,128)S(1)}, f32[1,1024]{1,0:T(1,128)S(1)}, f32[1,1024,128]{2,1,0:T(8,128)S(1)}, s32[1024]{0:T(1024)S(1)}, /*inde...) while((s32[]{:T(128)}, f32[1,1024]{1,0:T(1,128)S(1)}, ...), condition=%wide.region_7.7_spmd.clone, body=%wide.region_4.6_spmd.clone.sunk | while | flops 137430528 | bytes 4051139 | solution.py:72
  220.7 2.5 fusion.59
  224.0 11.6 %while.50 = (s32[]{:T(128)}, f32[1,1024]{1,0:T(1,128)S(1)}, f32[1,1024]{1,0:T(1,128)S(1)}, f32[1,1024,128]{2,1,0:T(8,128)S(1)}, s32[1024]{0:T(1024)S(1)}, /*inde...) while((s32[]{:T(128)}, f32[1,1024]{1,0:T(1,128)S(1)}, ...), condition=%wide.region_7.7_spmd.clone, body=%wide.region_4.6_spmd.clone.sunk | while | flops 137430528 | bytes 4051139 | solution.py:72
  235.7 2.5 fusion.59
  239.0 11.6 %while.50 = (s32[]{:T(128)}, f32[1,1024]{1,0:T(1,128)S(1)}, f32[1,1024]{1,0:T(1,128)S(1)}, f32[1,1024,128]{2,1,0:T(8,128)S(1)}, s32[1024]{0:T(1024)S(1)}, /*inde...) while((s32[]{:T(128)}, f32[1,1024]{1,0:T(1,128)S(1)}, ...), condition=%wide.region_7.7_spmd.clone, body=%wide.region_4.6_spmd.clone.sunk | while | flops 137430528 | bytes 4051139 | solution.py:72
  250.7 2.5 fusion.59
  254.1 8.0 %while.50 = (s32[]{:T(128)}, f32[1,1024]{1,0:T(1,128)S(1)}, f32[1,1024]{1,0:T(1,128)S(1)}, f32[1,1024,128]{2,1,0:T(8,128)S(1)}, s32[1024]{0:T(1024)S(1)}, /*inde...) while((s32[]{:T(128)}, f32[1,1024]{1,0:T(1,128)S(1)}, ...), condition=%wide.region_7.7_spmd.clone, body=%wide.region_4.6_spmd.clone.sunk | while | flops 137430528 | bytes 4051139 | solution.py:72
  262.0 2.5 fusion.59
  265.4 8.0 %while.50 = (s32[]{:T(128)}, f32[1,1024]{1,0:T(1,128)S(1)}, f32[1,1024]{1,0:T(1,128)S(1)}, f32[1,1024,128]{2,1,0:T(8,128)S(1)}, s32[1024]{0:T(1024)S(1)}, /*inde...) while((s32[]{:T(128)}, f32[1,1024]{1,0:T(1,128)S(1)}, ...), condition=%wide.region_7.7_spmd.clone, body=%wide.region_4.6_spmd.clone.sunk | while | flops 137430528 | bytes 4051139 | solution.py:72
  276.8 4.3 %while.50 = (s32[]{:T(128)}, f32[1,1024]{1,0:T(1,128)S(1)}, f32[1,1024]{1,0:T(1,128)S(1)}, f32[1,1024,128]{2,1,0:T(8,128)S(1)}, s32[1024]{0:T(1024)S(1)}, /*inde...) while((s32[]{:T(128)}, f32[1,1024]{1,0:T(1,128)S(1)}, ...), condition=%wide.region_7.7_spmd.clone, body=%wide.region_4.6_spmd.clone.sunk | while | flops 137430528 | bytes 4051139 | solution.py:72
  284.4 4.3 %while.50 = (s32[]{:T(128)}, f32[1,1024]{1,0:T(1,128)S(1)}, f32[1,1024]{1,0:T(1,128)S(1)}, f32[1,1024,128]{2,1,0:T(8,128)S(1)}, s32[1024]{0:T(1024)S(1)}, /*inde...) while((s32[]{:T(128)}, f32[1,1024]{1,0:T(1,128)S(1)}, ...), condition=%wide.region_7.7_spmd.clone, body=%wide.region_4.6_spmd.clone.sunk | while | flops 137430528 | bytes 4051139 | solution.py:72
  288.9 14.5 %all_to_all.10 = bf16[32,32,128]{2,1,0:T(8,128)(2,1)S(1)} all-to-all(bf16[32,32,128]{2,1,0:T(8,128)(2,1)S(1)} %bitcast.90), channel_id=1, replica_groups=mesh['ctx'=32,'tp'=8] {'ctx'}, dimensions={0} | all-to-all | bytes 524288 | tf_op jit(solution)/shard_map/all_to_all | solution.py:152
  303.4 4.9 %fusion.24 = bf16[256,4096]{1,0:T(8,128)(2,1)} fusion(bf16[4,256,128]{2,1,0:T(8,128)(2,1)S(1)} %bitcast.96, bf16[4,128,4096]{2,1,0:T(8,128)(2,1)} %bitcast.97), kind=kOutput, calls=%fused_computation.37 | convolution fusion | flops 1074790400 | bytes 6553600 | tf_op jit(solution)/shard_map/htk,hkd->td/dot_general | solution.py:154
  308.3 58.5 %reduce-scatter.2.cloned.1.call-done = bf16[256,512]{1,0:T(8,128)(2,1)} async-done(((bf16[256,4096]{1,0:T(8,128)(2,1)}), bf16[256,512]{1,0:T(8,128)(2,1)}) %reduce-scatter.2.cloned.1.call-update) | async-done | bytes 262160 | tf_op jit(solution)/shard_map/reduce_scatter | solution.py:160
  (247 shorter events, 45.1 us)
Async XLA Ops:
  6.5 45.7 %copy-start = (bf16[4096,128]{1,0:T(8,128)(2,1)S(1)}, bf16[4096,128]{1,0:T(8,128)(2,1)}, u32[]{:S(2)}) copy-start(bf16[4096,128]{1,0:T(8,128)(2,1)} %param.13) | copy-start | bytes 3145732
  6.5 43.4 %all-gather.3.cloned.1.call-start = ((), (), s32[]{:S(2)}) async-start(), calls=%async_computation.3 | async-start | bytes 2359296 | tf_op jit(solution)/shard_map/all_gather | solution.py:91
  7.3 169.6 %all-gather.5.cloned.1.call-start = ((), (), s32[]{:S(2)}) async-start(), calls=%async_computation.4 | async-start | bytes 4325376 | tf_op jit(solution)/shard_map/all_gather | solution.py:146
  50.0 5.1 %copy-start.1 = (bf16[256,4096]{1,0:T(8,128)(2,1)S(1)}, bf16[256,4096]{1,0:T(8,128)(2,1)}, u32[]{:S(2)}) copy-start(bf16[256,4096]{1,0:T(8,128)(2,1)} %all-gather.3.cloned.1.call-done) | copy-start | bytes 6291460
  50.0 5.1 %copy-start.2 = (bf16[4096,128]{1,0:T(8,128)(2,1)S(1)}, bf16[4096,128]{1,0:T(8,128)(2,1)}, u32[]{:S(2)}) copy-start(bf16[4096,128]{1,0:T(8,128)(2,1)} %param.14) | copy-start | bytes 3145732
  62.5 120.7 %all-to-all-start = ((bf16[32,32,128]{2,1,0:T(8,128)(2,1)}), bf16[32,32,128]{2,1,0:T(8,128)(2,1)S(1)}, u32[]{:S(2)}, u32[]{:S(2)}) async-start(bf16[32,32,128]{2,1,0:T(8,128)(2,1)} %pad_maximum_fusion), calls=%async_computation | async-start | bytes 524288 | tf_op jit(solution)/shard_map/all_to_all | solution.py:129
  69.3 297.5 %reduce-scatter.2.cloned.1.call-start = ((), (), s32[]{:S(2)}) async-start(), calls=%async_computation.5 | async-start | bytes 2359296 | tf_op jit(solution)/shard_map/reduce_scatter | solution.py:160
Sparse Core Ops, SparseCore 0:
  9.2 40.7 all-gather.2
  56.9 119.9 all-gather.4
  308.5 58.3 reduce-scatter.1
where the time goes:
time: 376 us; the launch traced here: 373 us
  waiting for transfers between devices  208 us (55%)
  loops' own time  53.2 us (14%)
  local copies, waits for them, and re-layouts  29.3 us (8%)
  matrix products  28 us (7%)
  other arithmetic  19.9 us (5%)
  blocking collectives  14.5 us (4%)
  between operations  13.3 us (4%)
  starting transfers between devices  6.89 us (2%)
    all_gather x1, waiting for transfers between devices, body(): lax.all_gather(kv_stack, 'ctx', axis=2, tiled=True)  107 us
    reduce_scatter x1, waiting for transfers between devices, body(): lax.psum_scatter(group_term.astype(jnp.bfloat16), 'tp', scatter_dimension...  58.5 us
    another operation x8, loops' own time, advance(): return lax.fori_loop(start_group, group_count, per_group, running)  52.8 us
    all_gather x1, waiting for transfers between devices, body(): gathered = lax.all_gather(tokens, 'tp', axis=1, tiled=True)  41.9 us
    slice x8, local copies, waits for them, and re-layouts, advance(): value_block = lax.dynamic_slice_in_dim(shard_rows[1], offset, block_rows, 1)  20 us
    all_to_all x1, blocking collectives, body(): lax.all_to_all(result, 'ctx', split_axis=0, concat_axis=0, tiled=True)  14.5 us
    dot_general x20, matrix products, per_group(): jnp.einsum('brk,bnk->brn', group_query, key_block, preferred_element_type...  7.8 us
    dot_general x20, matrix products, per_group(): jnp.einsum('brn,bnk->brk', weights.astype(jnp.bfloat16), value_block, pre...  7.69 us
  transfers between devices with their start and end apart: 4, of which 3 were waited for; matrix products, arithmetic and copies ran while one was open for 3% of the time, Pallas kernels for 0%

commit v1 on v0

v1 whole, which is shorter than its diff:
```python
import functools

import jax
import jax.numpy as jnp
from jax import lax
from jax.experimental import pallas as pl
from jax.experimental.pallas import tpu as pltpu
from jax.sharding import PartitionSpec as P

HEAD_DIM = 128
MESH = pl.DeviceIdType.MESH
ROWS = 256
HALF = 128
WIDTH = 4096
NC = 8
R = ROWS // NC
NS = 26
ND = 4
CR = ROWS // ND
MS = 6
CHUNK_KEYS = 8 * R
LOG2E = 1.4426950408889634


def device_at(x, y, z_hi, z_lo, core):
    return ((y % 4) * 8 + z_lo * 4 + x % 4, (z_hi % 4) * 2 + core)


def sublayer(
    tok, gain, cosine, sine, wq, wk, wv, wo, out,
    gathered, wqkv, wov, kv, q_here, q_away, top, denom, acc, att,
    term_away, term_in, term_own, relay_out, relay_in, fin_out, fin_in, back,
    w_sem, c_send, c_recv, d_send, d_recv,
):
    ctx = lax.axis_index("ctx")
    tp = lax.axis_index("tp")
    x, y, z_lo = ctx % 4, ctx // 8, (ctx // 4) % 2
    z_hi, core = tp // 2, tp % 2
    z_up = device_at(x, y, z_hi + 1, z_lo, core)
    z_down = device_at(x, y, z_hi + 3, z_lo, core)
    sibling = device_at(x, y, z_hi, z_lo, 1 - core)
    z_pair = device_at(x, y, z_hi, 1 - z_lo, core)
    x_up = device_at(x + 1, y, z_hi, z_lo, core)
    x_down = device_at(x + 3, y, z_hi, z_lo, core)
    y_up = device_at(x, y + 1, z_hi, z_lo, core)
    y_down = device_at(x, y + 3, z_hi, z_lo, core)
    partner = device_at(x, 3 - y, z_hi, z_lo, core)

    weights = [
        pltpu.make_async_copy(wq, wqkv.at[:, pl.ds(0, 512)], w_sem.at[0]),
        pltpu.make_async_copy(wk, wqkv.at[:, pl.ds(512, 128)], w_sem.at[1]),
        pltpu.make_async_copy(wv, wqkv.at[:, pl.ds(640, 128)], w_sem.at[2]),
        pltpu.make_async_copy(wo, wov, w_sem.at[3]),
    ]
    for copy in weights:
        copy.start()
    gathered[tp] = tok[...]

    barrier = pltpu.get_barrier_semaphore()
    peers = (z_up, z_down, sibling, z_pair, x_up, x_down, y_up, y_down)
    for peer in peers:
        pl.semaphore_signal(barrier, inc=1, device_id=peer, device_id_type=MESH)
    pl.semaphore_wait(barrier, len(peers))

    x_lo, x_hi, y_lo, y_hi = (x + 3) % 4, (x + 1) % 4, (y + 3) % 4, (y + 1) % 4

    def copy_c(number, c):
        rows = pl.ds(pl.multiple_of(c * R, R), R)
        first = pl.ds(pl.multiple_of(c * R, R // 2), R // 2)
        second = pl.ds(pl.multiple_of(c * R + R // 2, R // 2), R // 2)
        places = [
            lambda: (gathered.at[tp, rows], z_up),
            lambda: (gathered.at[tp, rows], z_down),
            lambda: (gathered.at[tp, rows], sibling),
            lambda: (gathered.at[(tp + 6) % 8, first], z_up),
            lambda: (gathered.at[(tp + 2) % 8, second], z_down),
            lambda: (gathered.at[(tp + 6) % 8, rows], sibling),
            lambda: (gathered.at[(tp + 2) % 8, rows], sibling),
            lambda: (gathered.at[(tp + 4) % 8, rows], sibling),
            lambda: (kv.at[:, c, y, x, z_lo], z_pair),
            lambda: (kv.at[0, c, y, x], x_up),
            lambda: (kv.at[0, c, y, x], x_down),
            lambda: (kv.at[0, c, y, x_lo, 0], x_up),
            lambda: (kv.at[0, c, y, x_hi, 1], x_down),
            lambda: (kv.at[0, c, y], y_up),
            lambda: (kv.at[0, c, y], y_down),
            lambda: (kv.at[0, c, y_lo, pl.ds(0, 2)], y_up),
            lambda: (kv.at[0, c, y_hi, pl.ds(2, 2)], y_down),
            lambda: (kv.at[1, c, y, x], y_up),
            lambda: (kv.at[1, c, y, x], y_down),
            lambda: (kv.at[1, c, y_lo, x, 0], y_up),
            lambda: (kv.at[1, c, y_hi, x, 1], y_down),
            lambda: (kv.at[1, c, :, x], x_up),
            lambda: (kv.at[1, c, :, x], x_down),
            lambda: (kv.at[1, c, pl.ds(0, 2), x_lo], x_up),
            lambda: (kv.at[1, c, pl.ds(2, 2), x_hi], x_down),
        ]
        if number < 25:
            place, target = places[number]()
            source = place
        else:
            rest = pl.ds(pl.multiple_of((c - NC // 2) * R, R), R)
            source, place, target = q_away.at[:, rest], q_here.at[0, :, rest], partner
        return pltpu.make_async_remote_copy(
            src_ref=source, dst_ref=place, send_sem=c_send.at[c, number], recv_sem=c_recv.at[c, number],
            device_id=target, device_id_type=MESH,
        )

    def start(numbers, c):
        for number in numbers:
            copy_c(number, c).start()

    def arrive(numbers, c):
        for number in numbers:
            copy_c(number, c).wait_recv()

    def rotate(field, cos_rows, sin_rows):
        return field * cos_rows + pltpu.roll(field, HEAD_DIM // 2, 1) * sin_rows

    def project(c):
        rows = pl.ds(pl.multiple_of(c * R, R), R)
        squares = jnp.zeros((R, 512), jnp.float32)
        for piece in range(8):
            values = gathered[piece, rows].astype(jnp.float32)
            squares = squares + values * values
        scale = lax.rsqrt(jnp.sum(squares, axis=1, keepdims=True) * (1.0 / WIDTH) + 1e-05)
        total = jnp.zeros((R, 768), jnp.float32)
        for piece in range(8):
            values = gathered[piece, rows].astype(jnp.float32)
            normed = (values * scale * gain[:, piece * 512:(piece + 1) * 512].astype(jnp.float32)).astype(jnp.bfloat16)
            total = total + jnp.dot(
                normed, wqkv[piece * 512:(piece + 1) * 512, :], preferred_element_type=jnp.float32
            )
        cos_rows, sin_rows = cosine[rows], sine[rows]
        kv[0, c, y, x, z_lo] = rotate(total[:, 512:640], cos_rows, sin_rows).astype(jnp.bfloat16)
        kv[1, c, y, x, z_lo] = total[:, 640:768].astype(jnp.bfloat16)
        queries = [
            rotate(total[:, h * 128:(h + 1) * 128], cos_rows, sin_rows).astype(jnp.bfloat16) for h in range(4)
        ]

        @pl.when(c < NC // 2)
        def _():
            for h in range(4):
                q_here[1, h, rows] = queries[h]

        @pl.when(c >= NC // 2)
        def _():
            rest = pl.ds(pl.multiple_of((c - NC // 2) * R, R), R)
            for h in range(4):
                q_away[h, rest] = queries[h]

    top[...] = jnp.full(top.shape, -1e30, jnp.float32)
    denom[...] = jnp.zeros(denom.shape, jnp.float32)
    acc[...] = jnp.zeros(acc.shape, jnp.float32)
    factor_log = LOG2E / HEAD_DIM ** 0.5

    def fold(c, half, group, masked):
        keys = kv[0, c, group].reshape(CHUNK_KEYS, HEAD_DIM)
        values = kv[1, c, group].reshape(CHUNK_KEYS, HEAD_DIM)
        queries = q_here[half].reshape(4 * HALF, HEAD_DIM)
        scores = lax.dot_general(
            queries, keys, (((1,), (1,)), ((), ())), preferred_element_type=jnp.float32
        )
        if masked:
            row = lax.broadcasted_iota(jnp.int32, (4 * HALF, 1), 0) % HALF + (1 - half) * HALF
            column = lax.broadcasted_iota(jnp.int32, (1, CHUNK_KEYS), 1)
            block = (column // R) % 2 * 4 + column // (2 * R)
            key_row = (block - (z_lo * 4 + x)) * ROWS + c * R + column % R
            scores = jnp.where(key_row <= row, scores, -2e30)
        old = top[half]
        newest = jnp.maximum(old, jnp.max(scores, axis=1, keepdims=True))
        top[half] = newest
        shrink = jnp.exp2((old - newest) * factor_log)
        wide = jnp.concatenate([newest] * (CHUNK_KEYS // 128), axis=1)
        weights = jnp.exp2((scores - wide) * factor_log)
        part = weights[:, 0:128]
        for at in range(1, CHUNK_KEYS // 128):
            part = part + weights[:, at * 128:(at + 1) * 128]
        denom[half] = denom[half] * shrink + part
        acc[half] = acc[half] * shrink + jnp.dot(
            weights.astype(jnp.bfloat16), values, preferred_element_type=jnp.float32
        )

    def attend(c):
        groups_away = 3 - y

        def body(step, carry):
            half = (step >= groups_away).astype(jnp.int32)
            group = step - half * groups_away
            fold(c, half, group, False)
            return carry

        lax.fori_loop(0, 3, body, 0)

        def diagonal(half, carry):
            fold(c, half, jnp.where(half == 0, 3 - y, y), True)
            return carry

        lax.fori_loop(0, 2, diagonal, 0)

    start((0, 1, 2), 0)
    start((0, 1, 2), 1)

    def tick(t, carry):
        @pl.when((t >= 5) & (t < NC + 5))
        def _():
            arrive((13, 14), t - 5)
            start((15, 16), t - 5)
            arrive((21, 22), t - 5)
            start((23, 24), t - 5)

        @pl.when((t >= 4) & (t < NC + 4))
        def _():
            arrive((11, 12), t - 4)
            start((13, 14), t - 4)
            arrive((19, 20), t - 4)
            start((21, 22), t - 4)

        @pl.when((t >= 3) & (t < NC + 3))
        def _():
            arrive((9, 10), t - 3)
            start((11, 12), t - 3)
            arrive((17, 18), t - 3)
            start((19, 20), t - 3)

        @pl.when((t >= 2) & (t < NC + 2))
        def _():
            arrive((8,), t - 2)
            start((9, 10, 17, 18), t - 2)

        @pl.when(t < NC)
        def _():
            arrive((0, 1), t)
            start((3, 4, 5, 6), t)

        @pl.when(t + 2 < NC)
        def _():
            start((0, 1, 2), t + 2)

        @pl.when(t == 1)
        def _():
            for copy in weights[:3]:
                copy.wait()

        @pl.when((t >= 1) & (t < NC + 1))
        def _():
            arrive((2, 5, 6, 7), t - 1)
            project(t - 1)
            start((8,), t - 1)

        @pl.when((t >= NC // 2 + 1) & (t < NC + 1))
        def _():
            start((25,), t - 1)

        @pl.when(t < NC)
        def _():
            arrive((3, 4), t)
            start((7,), t)

        @pl.when(t == NC)
        def _():
            for c in range(NC // 2, NC):
                arrive((25,), c)

        @pl.when(t >= NC)
        def _():
            arrive((15, 16, 23, 24), t - NC)
            attend(t - NC)

        return carry

    lax.fori_loop(0, 2 * NC, tick, 0)

    for half in range(2):
        whole = acc[half] / jnp.sum(denom[half], axis=1, keepdims=True)
        for h in range(4):
            att[half * HALF:(half + 1) * HALF, h * 128:(h + 1) * 128] = whole[
                h * HALF:(h + 1) * HALF
            ].astype(jnp.bfloat16)
    weights[3].wait()

    def copy_d(number, u):
        return pltpu.make_async_remote_copy(
            **dict(zip(("src_ref", "dst_ref", "device_id"), (
                lambda: (term_away.at[u], term_in.at[u], sibling),
                lambda: (relay_out.at[0, u], relay_in.at[0, u], z_up),
                lambda: (relay_out.at[1, u], relay_in.at[1, u], z_down),
                lambda: (fin_out.at[0, u], fin_in.at[0, u], z_up),
                lambda: (fin_out.at[1, u], fin_in.at[1, u], z_down),
                lambda: (
                    back.at[pl.ds(pl.multiple_of(u * CR, CR), CR)],
                    out.at[pl.ds(pl.multiple_of(HALF + u * CR, CR), CR)],
                    partner,
                ),
            )[number]())),
            send_sem=d_send.at[u, number], recv_sem=d_recv.at[u, number], device_id_type=MESH,
        )

    def term(u, column):
        return jnp.dot(
            att[pl.ds(pl.multiple_of(u * CR, CR), CR)],
            wov[:, pl.ds(pl.multiple_of(column * 512, 512), 512)],
            preferred_element_type=jnp.float32,
        ).astype(jnp.bfloat16)

    def paired(u, at, rows):
        return term_own[u, at, rows].astype(jnp.float32) + term_in[u, at, rows].astype(jnp.float32)

    low, high = pl.ds(0, CR // 2), pl.ds(CR // 2, CR // 2)
    opposite, above, below = (z_hi + 2) % 4, (z_hi + 1) % 4, (z_hi + 3) % 4

    def out_tick(u, carry):
        @pl.when(u < ND)
        def _():
            for at in range(4):
                term_away[u, at] = term(u, at * 2 + 1 - core)
            copy_d(0, u).start()
            for at in range(4):
                term_own[u, at] = term(u, at * 2 + core)
            copy_d(0, u).wait_recv()
            relay_out[0, u] = paired(u, opposite, low).astype(jnp.bfloat16)
            copy_d(1, u).start()
            relay_out[1, u] = paired(u, opposite, high).astype(jnp.bfloat16)
            copy_d(2, u).start()

        @pl.when((u >= 1) & (u < ND + 1))
        def _():
            v = u - 1
            copy_d(1, v).wait_recv()
            fin_out[0, v, low] = (paired(v, above, low) + relay_in[0, v].astype(jnp.float32)).astype(jnp.bfloat16)
            fin_out[0, v, high] = paired(v, above, high).astype(jnp.bfloat16)
            copy_d(3, v).start()
            copy_d(2, v).wait_recv()
            fin_out[1, v, low] = paired(v, below, low).astype(jnp.bfloat16)
            fin_out[1, v, high] = (paired(v, below, high) + relay_in[1, v].astype(jnp.float32)).astype(jnp.bfloat16)
            copy_d(4, v).start()

        @pl.when(u >= 2)
        def _():
            v = u - 2
            copy_d(3, v).wait_recv()
            copy_d(4, v).wait_recv()
            whole = (
                paired(v, z_hi, pl.ds(0, CR)) + fin_in[0, v].astype(jnp.float32) + fin_in[1, v].astype(jnp.float32)
            ).astype(jnp.bfloat16)

            @pl.when(v < ND // 2)
            def _():
                back[pl.ds(pl.multiple_of(v * CR, CR), CR)] = whole
                copy_d(5, v).start()

            @pl.when(v >= ND // 2)
            def _():
                out[pl.ds(pl.multiple_of(v * CR - HALF, CR), CR)] = whole

        return carry

    lax.fori_loop(0, ND + 2, out_tick, 0)

    def drain_c(c, carry):
        for number in range(25):
            copy_c(number, c).wait_send()
        return carry

    def drain_q(c, carry):
        copy_c(25, c).wait_send()
        return carry

    def drain_d(u, carry):
        for number in range(5):
            copy_d(number, u).wait_send()
        return carry

    def drain_y(u, carry):
        copy_d(5, u).wait()
        return carry

    lax.fori_loop(0, NC, drain_c, 0)
    lax.fori_loop(NC // 2, NC, drain_q, 0)
    lax.fori_loop(0, ND, drain_d, 0)
    lax.fori_loop(0, ND // 2, drain_y, 0)


def body(tokens, norm_gain, w_query, w_key, w_value, w_output):
    half = HEAD_DIM // 2
    frequency = 500000.0 ** (-2.0 * jnp.arange(half, dtype=jnp.float32) / HEAD_DIM)
    positions = lax.axis_index("ctx") * ROWS + jnp.arange(ROWS, dtype=jnp.int32)
    angles = positions.astype(jnp.float32)[:, None] * frequency[None, :]
    cosine = jnp.cos(angles)
    sine = jnp.sin(angles)
    cosine = jnp.concatenate([cosine, cosine], axis=1)
    sine = jnp.concatenate([-sine, sine], axis=1)
    vmem = pl.BlockSpec(memory_space=pltpu.VMEM)
    hbm = pl.BlockSpec(memory_space=pl.ANY)
    bf16, f32 = jnp.bfloat16, jnp.float32
    return pl.pallas_call(
        sublayer,
        out_shape=jax.ShapeDtypeStruct((ROWS, 512), bf16),
        in_specs=[vmem] * 4 + [hbm] * 4,
        out_specs=vmem,
        scratch_shapes=[
            pltpu.VMEM((8, ROWS, 512), bf16),
            pltpu.VMEM((WIDTH, 768), bf16),
            pltpu.VMEM((512, WIDTH), bf16),
            pltpu.VMEM((2, NC, 4, 4, 2, R, HEAD_DIM), bf16),
            pltpu.VMEM((2, 4, HALF, HEAD_DIM), bf16),
            pltpu.VMEM((4, HALF, HEAD_DIM), bf16),
            pltpu.VMEM((2, 4 * HALF, 128), f32),
            pltpu.VMEM((2, 4 * HALF, 128), f32),
            pltpu.VMEM((2, 4 * HALF, HEAD_DIM), f32),
            pltpu.VMEM((ROWS, 512), bf16),
            pltpu.VMEM((ND, 4, CR, 512), bf16),
            pltpu.VMEM((ND, 4, CR, 512), bf16),
            pltpu.VMEM((ND, 4, CR, 512), bf16),
            pltpu.VMEM((2, ND, CR // 2, 512), bf16),
            pltpu.VMEM((2, ND, CR // 2, 512), bf16),
            pltpu.VMEM((2, ND, CR, 512), bf16),
            pltpu.VMEM((2, ND, CR, 512), bf16),
            pltpu.VMEM((HALF, 512), bf16),
            pltpu.SemaphoreType.DMA((4,)),
            pltpu.SemaphoreType.DMA((NC, NS)),
            pltpu.SemaphoreType.DMA((NC, NS)),
            pltpu.SemaphoreType.DMA((ND, MS)),
            pltpu.SemaphoreType.DMA((ND, MS)),
        ],
        compiler_params=pltpu.CompilerParams(
            collective_id=0, has_side_effects=True, vmem_limit_bytes=52 << 20
        ),
        cost_estimate=pl.CostEstimate(flops=6_000_000_000, bytes_accessed=12_000_000, transcendentals=6_000_000),
    )(tokens, norm_gain.reshape(1, WIDTH), cosine, sine, w_query, w_key, w_value, w_output)


def solution(mesh):
    placed = (P("ctx", "tp"), P(), P(None, "tp"), P(None, "tp"), P(None, "tp"), P("tp", None))
    return jax.shard_map(
        body, mesh=mesh, in_specs=placed, out_specs=P("ctx", "tp"), check_vma=False
    )
```

time: 376 us -> 115 us (0.31)
  waiting for transfers between devices: 208 us -> 0 us
  Pallas kernels: 0 us -> 111 us
  loops' own time: 53.2 us -> 0 us
  matrix products: 28 us -> 0 us
  local copies, waits for them, and re-layouts: 29.3 us -> 3.58 us
  other arithmetic: 19.9 us -> 0.69 us
  blocking collectives: 14.5 us -> 0 us
  between operations: 13.3 us -> 0.04 us
  starting transfers between devices: 6.89 us -> 0 us
    all_gather x2 -> x0, waiting for transfers between devices: 149 us -> none  [the longest x1 107 us: body(): lax.all_gather(kv_stack, 'ctx', axis=2, tiled=True)]
    pallas_call x0 -> x1, Pallas kernels: none -> 111 us  [body(): pl.pallas_call(sublayer, out_shape=jax.ShapeDtypeStruct((ROWS, 512), bf16...]
    reduce_scatter x1 -> x0, waiting for transfers between devices: 58.5 us -> none  [body(): lax.psum_scatter(group_term.astype(jnp.bfloat16), 'tp', scatter_dimension...]
    another operation x9 -> x0, loops' own time: 53.2 us -> none  [the longest x8 52.8 us: advance(): return lax.fori_loop(start_group, group_count, per_group, running)]
    dot_general x43 -> x0, matrix products: 23.9 us -> none  [the longest x20 7.8 us: per_group(): jnp.einsum('brk,bnk->brn', group_query, key_block, preferred_element_type...]
    slice x8 -> x0, local copies, waits for them, and re-layouts: 20 us -> none  [advance(): value_block = lax.dynamic_slice_in_dim(shard_rows[1], offset, block_rows, 1)]
    reduce_sum x29 -> x0, other arithmetic: 15.1 us -> none  [the longest x20 7.52 us: per_group(): denominator = denominator * factor + jnp.sum(weights, axis=-1)]
    all_to_all x1 -> x0, blocking collectives: 14.5 us -> none  [body(): lax.all_to_all(result, 'ctx', split_axis=0, concat_axis=0, tiled=True)]
  transfers between devices with their start and end apart: 4 -> 0, of which waited for: 3 -> 0; matrix products, arithmetic and copies ran while one was open for 3% -> 0% of each run, Pallas kernels for 0% -> 0%
where the time goes in v1:
time: 115 us
  Pallas kernels  111 us (97%)
  local copies, waits for them, and re-layouts  3.58 us (3%)
    pallas_call x1, Pallas kernels, body(): pl.pallas_call(sublayer, out_shape=jax.ShapeDtypeStruct((ROWS, 512), bf16...  111 us
    unnamed x5, local copies, waits for them, and re-layouts  2.87 us

profile of v1, /device:TPU:1, one launch (start us, length us, event | category | flops | bytes accessed | tf_op | source)
XLA Modules:
  0.0 115.3 jit_solution(4859435715597828952)
XLA Ops:
  0.0 0.5 fusion
  0.6 0.1 pad_maximum_fusion
  0.7 0.7 reshape.13.gain
  1.4 0.0 copy-start
  1.4 1.2 %copy-done = bf16[4096,128]{1,0:T(8,128)(2,1)S(1)} copy-done((bf16[4096,128]{1,0:T(8,128)(2,1)S(1)}, bf16[4096,128]{1,0:T(8,128)(2,1)}, u32[]{:S(2)}) %copy-start) | copy-done | bytes 1048600
  2.6 0.0 copy-start.1
  2.6 0.9 copy-done.1
  3.6 111.0 %shard_map.64 = bf16[256,512]{1,0:T(8,128)(2,1)S(1)} custom-call(bf16[256,512]{1,0:T(8,128)(2,1)S(1)} %copy-done.1, bf16[1,4096]{1,0:T(2,128)(2,1)S(1)} %reshape.13.gain, f32[256,128]{1,0:T(8,128)S(1)} %get-tuple-element.8.cosine, f32[256,128]{1,0:T(8,128)S(1)} %get-tuple-element.9.sine, bf16[4096,512]{1,0:T(8,128)(2,1)} %wq.1, ...), custom_call_target="tpu_custom_call" | custom-call | flops 6000000000 | bytes 12000000 | tf_op jit(solution)/shard_map/pallas_call | solution.py:396
  114.6 0.7 copy.8
  (2 shorter events, 0.0 us)
Async XLA Ops:
  1.4 1.2 %copy-start = (bf16[4096,128]{1,0:T(8,128)(2,1)S(1)}, bf16[4096,128]{1,0:T(8,128)(2,1)}, u32[]{:S(2)}) copy-start(bf16[4096,128]{1,0:T(8,128)(2,1)} %wk.1) | copy-start | bytes 3145732
  2.6 0.9 copy-start.1

commit v2 on v1

--- a/solution.py
+++ b/solution.py
@@ -12,12 +12,16 @@
 ROWS = 256
 HALF = 128
 WIDTH = 4096
-NC = 8
+NC = 4
 R = ROWS // NC
 NS = 26
 ND = 4
 CR = ROWS // ND
 MS = 6
+AHEAD = 3
+A_DIRECT, P1_DIRECT, P2_DIRECT = False, False, False
+LAG_A3, LAG_P, LAG_S1, LAG_S2, LAG_S3, LAG_S4, LAG_ATT = 2, 3, 5, 7, 9, 11, 13
+LAG_D3, LAG_D4 = 1, 3
 CHUNK_KEYS = 8 * R
 LOG2E = 1.4426950408889634
 
@@ -52,14 +56,16 @@
         pltpu.make_async_copy(wv, wqkv.at[:, pl.ds(640, 128)], w_sem.at[2]),
         pltpu.make_async_copy(wo, wov, w_sem.at[3]),
     ]
+    own_tokens = pltpu.make_async_copy(tok, gathered.at[tp], w_sem.at[4])
+    own_tokens.start()
     for copy in weights:
         copy.start()
-    gathered[tp] = tok[...]
 
     barrier = pltpu.get_barrier_semaphore()
     peers = (z_up, z_down, sibling, z_pair, x_up, x_down, y_up, y_down)
     for peer in peers:
         pl.semaphore_signal(barrier, inc=1, device_id=peer, device_id_type=MESH)
+    own_tokens.wait()
     pl.semaphore_wait(barrier, len(peers))
 
     x_lo, x_hi, y_lo, y_hi = (x + 3) % 4, (x + 1) % 4, (y + 3) % 4, (y + 1) % 4
@@ -68,11 +74,15 @@
         rows = pl.ds(pl.multiple_of(c * R, R), R)
         first = pl.ds(pl.multiple_of(c * R, R // 2), R // 2)
         second = pl.ds(pl.multiple_of(c * R + R // 2, R // 2), R // 2)
+        x_far = device_at(x + 2, y, z_hi, z_lo, core)
+        y_far = device_at(x, y + 2, z_hi, z_lo, core)
+        z_far = device_at(x, y, z_hi + 2, z_lo, core)
         places = [
             lambda: (gathered.at[tp, rows], z_up),
             lambda: (gathered.at[tp, rows], z_down),
             lambda: (gathered.at[tp, rows], sibling),
-            lambda: (gathered.at[(tp + 6) % 8, first], z_up),
+            (lambda: (gathered.at[tp, rows], z_far)) if A_DIRECT
+            else (lambda: (gathered.at[(tp + 6) % 8, first], z_up)),
             lambda: (gathered.at[(tp + 2) % 8, second], z_down),
             lambda: (gathered.at[(tp + 6) % 8, rows], sibling),
             lambda: (gathered.at[(tp + 2) % 8, rows], sibling),
@@ -80,19 +90,23 @@
             lambda: (kv.at[:, c, y, x, z_lo], z_pair),
             lambda: (kv.at[0, c, y, x], x_up),
             lambda: (kv.at[0, c, y, x], x_down),
-            lambda: (kv.at[0, c, y, x_lo, 0], x_up),
+            (lambda: (kv.at[0, c, y, x], x_far)) if P1_DIRECT
+            else (lambda: (kv.at[0, c, y, x_lo, 0], x_up)),
             lambda: (kv.at[0, c, y, x_hi, 1], x_down),
             lambda: (kv.at[0, c, y], y_up),
             lambda: (kv.at[0, c, y], y_down),
-            lambda: (kv.at[0, c, y_lo, pl.ds(0, 2)], y_up),
+            (lambda: (kv.at[0, c, y], y_far)) if P2_DIRECT
+            else (lambda: (kv.at[0, c, y_lo, pl.ds(0, 2)], y_up)),
             lambda: (kv.at[0, c, y_hi, pl.ds(2, 2)], y_down),
             lambda: (kv.at[1, c, y, x], y_up),
             lambda: (kv.at[1, c, y, x], y_down),
-            lambda: (kv.at[1, c, y_lo, x, 0], y_up),
+            (lambda: (kv.at[1, c, y, x], y_far)) if P1_DIRECT
+            else (lambda: (kv.at[1, c, y_lo, x, 0], y_up)),
             lambda: (kv.at[1, c, y_hi, x, 1], y_down),
             lambda: (kv.at[1, c, :, x], x_up),
             lambda: (kv.at[1, c, :, x], x_down),
-            lambda: (kv.at[1, c, pl.ds(0, 2), x_lo], x_up),
+            (lambda: (kv.at[1, c, :, x], x_far)) if P2_DIRECT
+            else (lambda: (kv.at[1, c, pl.ds(0, 2), x_lo], x_up)),
             lambda: (kv.at[1, c, pl.ds(2, 2), x_hi], x_down),
         ]
         if number < 25:
@@ -127,7 +141,7 @@
         total = jnp.zeros((R, 768), jnp.float32)
         for piece in range(8):
             values = gathered[piece, rows].astype(jnp.float32)
-            normed = (values * scale * gain[:, piece * 512:(piece + 1) * 512].astype(jnp.float32)).astype(jnp.bfloat16)
+            normed = (values * scale * gain[piece * 512:(piece + 1) * 512].astype(jnp.float32).reshape(1, 512)).astype(jnp.bfloat16)
             total = total + jnp.dot(
                 normed, wqkv[piece * 512:(piece + 1) * 512, :], preferred_element_type=jnp.float32
             )
@@ -198,78 +212,96 @@
 
         lax.fori_loop(0, 2, diagonal, 0)
 
-    start((0, 1, 2), 0)
-    start((0, 1, 2), 1)
+    own = (0, 1, 3, 2) if A_DIRECT else (0, 1, 2)
+    if P2_DIRECT:
+        spread, last = (13, 14, 15, 21, 22, 23), (13, 14, 15, 21, 22, 23)
+    else:
+        spread, last = (13, 14, 21, 22), (15, 16, 23, 24)
+    if P1_DIRECT:
+        near = (9, 10, 11, 17, 18, 19)
+    else:
+        near = (9, 10, 17, 18)
+
+    for c in range(AHEAD):
+        start(own, c)
+
+    def during(t, lag):
+        return (t >= lag) & (t < NC + lag)
 
     def tick(t, carry):
-        @pl.when((t >= 5) & (t < NC + 5))
-        def _():
-            arrive((13, 14), t - 5)
-            start((15, 16), t - 5)
-            arrive((21, 22), t - 5)
-            start((23, 24), t - 5)
-
-        @pl.when((t >= 4) & (t < NC + 4))
-        def _():
-            arrive((11, 12), t - 4)
-            start((13, 14), t - 4)
-            arrive((19, 20), t - 4)
-            start((21, 22), t - 4)
-
-        @pl.when((t >= 3) & (t < NC + 3))
-        def _():
-            arrive((9, 10), t - 3)
-            start((11, 12), t - 3)
-            arrive((17, 18), t - 3)
-            start((19, 20), t - 3)
-
-        @pl.when((t >= 2) & (t < NC + 2))
-        def _():
-            arrive((8,), t - 2)
-            start((9, 10, 17, 18), t - 2)
+        if not P2_DIRECT:
+            @pl.when(during(t, LAG_S4))
+            def _():
+                arrive((13, 14), t - LAG_S4)
+                start((15, 16), t - LAG_S4)
+                arrive((21, 22), t - LAG_S4)
+                start((23, 24), t - LAG_S4)
+
+        @pl.when(during(t, LAG_S3))
+        def _():
+            arrive(near if P1_DIRECT else (11, 12, 19, 20), t - LAG_S3)
+            start(spread, t - LAG_S3)
+
+        if not P1_DIRECT:
+            @pl.when(during(t, LAG_S2))
+            def _():
+                arrive((9, 10), t - LAG_S2)
+                start((11, 12), t - LAG_S2)
+                arrive((17, 18), t - LAG_S2)
+                start((19, 20), t - LAG_S2)
+
+        @pl.when(during(t, LAG_S1))
+        def _():
+            arrive((8,), t - LAG_S1)
+            start(near, t - LAG_S1)
+
+        if not A_DIRECT:
+            @pl.when(during(t, LAG_A3))
+            def _():
+                arrive((3, 4), t - LAG_A3)
+                start((7,), t - LAG_A3)
 
         @pl.when(t < NC)
         def _():
-            arrive((0, 1), t)
-            start((3, 4, 5, 6), t)
-
-        @pl.when(t + 2 < NC)
-        def _():
-            start((0, 1, 2), t + 2)
-
-        @pl.when(t == 1)
+            if A_DIRECT:
+                arrive((0, 1, 3), t)
+                start((5, 6, 7), t)
+            else:
+                arrive((0, 1), t)
+                start((3, 4, 5, 6), t)
+
+        @pl.when(t + AHEAD < NC)
+        def _():
+            start(own, t + AHEAD)
+
+        @pl.when(t == LAG_P)
         def _():
             for copy in weights[:3]:
                 copy.wait()
 
-        @pl.when((t >= 1) & (t < NC + 1))
-        def _():
-            arrive((2, 5, 6, 7), t - 1)
-            project(t - 1)
-            start((8,), t - 1)
-
-        @pl.when((t >= NC // 2 + 1) & (t < NC + 1))
-        def _():
-            start((25,), t - 1)
-
-        @pl.when(t < NC)
-        def _():
-            arrive((3, 4), t)
-            start((7,), t)
-
-        @pl.when(t == NC)
+        @pl.when(during(t, LAG_P))
+        def _():
+            arrive((2, 5, 6, 7), t - LAG_P)
+            project(t - LAG_P)
+            start((8,), t - LAG_P)
+
+        @pl.when((t >= NC // 2 + LAG_P) & (t < NC + LAG_P))
+        def _():
+            start((25,), t - LAG_P)
+
+        @pl.when(t == LAG_ATT)
         def _():
             for c in range(NC // 2, NC):
                 arrive((25,), c)
 
-        @pl.when(t >= NC)
-        def _():
-            arrive((15, 16, 23, 24), t - NC)
-            attend(t - NC)
-
-        return carry
-
-    lax.fori_loop(0, 2 * NC, tick, 0)
+        @pl.when(t >= LAG_ATT)
+        def _():
+            arrive(last, t - LAG_ATT)
+            attend(t - LAG_ATT)
+
+        return carry
+
+    lax.fori_loop(0, NC + LAG_ATT, tick, 0)
 
     for half in range(2):
         whole = acc[half] / jnp.sum(denom[half], axis=1, keepdims=True)
@@ -323,9 +355,9 @@
             relay_out[1, u] = paired(u, opposite, high).astype(jnp.bfloat16)
             copy_d(2, u).start()
 
-        @pl.when((u >= 1) & (u < ND + 1))
-        def _():
-            v = u - 1
+        @pl.when((u >= LAG_D3) & (u < ND + LAG_D3))
+        def _():
+            v = u - LAG_D3
             copy_d(1, v).wait_recv()
             fin_out[0, v, low] = (paired(v, above, low) + relay_in[0, v].astype(jnp.float32)).astype(jnp.bfloat16)
             fin_out[0, v, high] = paired(v, above, high).astype(jnp.bfloat16)
@@ -335,9 +367,9 @@
             fin_out[1, v, high] = (paired(v, below, high) + relay_in[1, v].astype(jnp.float32)).astype(jnp.bfloat16)
             copy_d(4, v).start()
 
-        @pl.when(u >= 2)
-        def _():
-            v = u - 2
+        @pl.when(u >= LAG_D4)
+        def _():
+            v = u - LAG_D4
             copy_d(3, v).wait_recv()
             copy_d(4, v).wait_recv()
             whole = (
@@ -355,11 +387,14 @@
 
         return carry
 
-    lax.fori_loop(0, ND + 2, out_tick, 0)
+    lax.fori_loop(0, ND + LAG_D4, out_tick, 0)
+
+    unused = ((4,) if A_DIRECT else ()) + ((12, 20) if P1_DIRECT else ()) + ((16, 24) if P2_DIRECT else ())
 
     def drain_c(c, carry):
         for number in range(25):
-            copy_c(number, c).wait_send()
+            if number not in unused:
+                copy_c(number, c).wait_send()
         return carry
 
     def drain_q(c, carry):
@@ -396,7 +431,7 @@
     return pl.pallas_call(
         sublayer,
         out_shape=jax.ShapeDtypeStruct((ROWS, 512), bf16),
-        in_specs=[vmem] * 4 + [hbm] * 4,
+        in_specs=[hbm] + [vmem] * 3 + [hbm] * 4,
         out_specs=vmem,
         scratch_shapes=[
             pltpu.VMEM((8, ROWS, 512), bf16),
@@ -417,17 +452,17 @@
             pltpu.VMEM((2, ND, CR, 512), bf16),
             pltpu.VMEM((2, ND, CR, 512), bf16),
             pltpu.VMEM((HALF, 512), bf16),
-            pltpu.SemaphoreType.DMA((4,)),
+            pltpu.SemaphoreType.DMA((5,)),
             pltpu.SemaphoreType.DMA((NC, NS)),
             pltpu.SemaphoreType.DMA((NC, NS)),
             pltpu.SemaphoreType.DMA((ND, MS)),
             pltpu.SemaphoreType.DMA((ND, MS)),
         ],
         compiler_params=pltpu.CompilerParams(
-            collective_id=0, has_side_effects=True, vmem_limit_bytes=52 << 20
+            collective_id=0, has_side_effects=True, vmem_limit_bytes=62 << 20
         ),
         cost_estimate=pl.CostEstimate(flops=6_000_000_000, bytes_accessed=12_000_000, transcendentals=6_000_000),
-    )(tokens, norm_gain.reshape(1, WIDTH), cosine, sine, w_query, w_key, w_value, w_output)
+    )(tokens, norm_gain, cosine, sine, w_query, w_key, w_value, w_output)
 
 
 def solution(mesh):

time: 115 us -> 97.2 us (0.85)
  Pallas kernels: 111 us -> 94 us
  local copies, waits for them, and re-layouts: 3.58 us -> 1.67 us
    pallas_call x1, Pallas kernels: 111 us -> 94 us  [body(): pl.pallas_call(sublayer, out_shape=jax.ShapeDtypeStruct((ROWS, 512), bf16...]
    unnamed x5 -> x1, local copies, waits for them, and re-layouts: 2.87 us -> 1.67 us
where the time goes in v2:
time: 97.2 us; the launch traced here: 97.1 us
  Pallas kernels  94 us (97%)
  local copies, waits for them, and re-layouts  1.67 us (2%)
  other arithmetic  1.39 us (1%)
    pallas_call x1, Pallas kernels, body(): pl.pallas_call(sublayer, out_shape=jax.ShapeDtypeStruct((ROWS, 512), bf16...  94 us

profile of v2, /device:TPU:1, one launch (start us, length us, event | category | flops | bytes accessed | tf_op | source)
XLA Modules:
  0.0 97.1 jit_solution(12759049108726131306)
XLA Ops:
  0.0 0.5 fusion
  0.6 0.8 pad_maximum_fusion
  1.4 94.0 %shard_map.64 = bf16[256,512]{1,0:T(8,128)(2,1)} custom-call(bf16[256,512]{1,0:T(8,128)(2,1)} %tok.1, bf16[4096]{0:T(1024)(128)(2,1)} %gain.1, f32[256,128]{1,0:T(8,128)} %get-tuple-element.8.cosine, f32[256,128]{1,0:T(8,128)} %get-tuple-element.9.sine, bf16[4096,512]{1,0:T(8,128)(2,1)} %wq.1, bf16[4096,128]{1,0:T(8,128)(2,1)} %wk.1, bf16[4096,128]{1,0:T(8,128)(2,1)} %wv.1, ...), custom_call_target="tpu_custom_call" | custom-call | flops 6000000000 | bytes 12000000 | tf_op jit(solution)/shard_map/pallas_call | solution.py:431
  95.4 1.7 %copy.8 = bf16[256,512]{1,0:T(8,128)(2,1)} copy(bf16[256,512]{1,0:T(8,128)(2,1)} %shard_map.64) | data formatting | bytes 524288
  (2 shorter events, 0.0 us)

commit v3 on v2

--- a/solution.py
+++ b/solution.py
@@ -14,15 +14,14 @@
 WIDTH = 4096
 NC = 4
 R = ROWS // NC
-NS = 26
+NS = 24
 ND = 4
 CR = ROWS // ND
 MS = 6
-AHEAD = 3
-A_DIRECT, P1_DIRECT, P2_DIRECT = False, False, False
-LAG_A3, LAG_P, LAG_S1, LAG_S2, LAG_S3, LAG_S4, LAG_ATT = 2, 3, 5, 7, 9, 11, 13
+AHEAD = 4
+LAG_S3, LAG_ATT = 2, 5
 LAG_D3, LAG_D4 = 1, 3
-CHUNK_KEYS = 8 * R
+CHUNK_KEYS = 4 * R
 LOG2E = 1.4426950408889634
 
 
@@ -34,7 +33,8 @@
     tok, gain, cosine, sine, wq, wk, wv, wo, out,
     gathered, wqkv, wov, kv, q_here, q_away, top, denom, acc, att,
     term_away, term_in, term_own, relay_out, relay_in, fin_out, fin_in, back,
-    w_sem, c_send, c_recv, d_send, d_recv,
+    part_out, part_in, log_out, log_in,
+    w_sem, c_send, c_recv, d_send, d_recv, o_send, o_recv,
 ):
     ctx = lax.axis_index("ctx")
     tp = lax.axis_index("tp")
@@ -49,6 +49,10 @@
     y_up = device_at(x, y + 1, z_hi, z_lo, core)
     y_down = device_at(x, y + 3, z_hi, z_lo, core)
     partner = device_at(x, 3 - y, z_hi, z_lo, core)
+    diagonal_peer = device_at(x, 3 - y, z_hi, 1 - z_lo, core)
+    x_far = device_at(x + 2, y, z_hi, z_lo, core)
+    y_far = device_at(x, y + 2, z_hi, z_lo, core)
+    z_far = device_at(x, y, z_hi + 2, z_lo, core)
 
     weights = [
         pltpu.make_async_copy(wq, wqkv.at[:, pl.ds(0, 512)], w_sem.at[0]),
@@ -62,59 +66,36 @@
         copy.start()
 
     barrier = pltpu.get_barrier_semaphore()
-    peers = (z_up, z_down, sibling, z_pair, x_up, x_down, y_up, y_down)
+    peers = (z_up, z_down, z_far, sibling, z_pair, diagonal_peer, x_up, x_down, x_far, y_up, y_down, y_far)
     for peer in peers:
         pl.semaphore_signal(barrier, inc=1, device_id=peer, device_id_type=MESH)
     own_tokens.wait()
     pl.semaphore_wait(barrier, len(peers))
 
-    x_lo, x_hi, y_lo, y_hi = (x + 3) % 4, (x + 1) % 4, (y + 3) % 4, (y + 1) % 4
-
     def copy_c(number, c):
         rows = pl.ds(pl.multiple_of(c * R, R), R)
-        first = pl.ds(pl.multiple_of(c * R, R // 2), R // 2)
-        second = pl.ds(pl.multiple_of(c * R + R // 2, R // 2), R // 2)
-        x_far = device_at(x + 2, y, z_hi, z_lo, core)
-        y_far = device_at(x, y + 2, z_hi, z_lo, core)
-        z_far = device_at(x, y, z_hi + 2, z_lo, core)
+        tokens = [gathered.at[(tp + back_by) % 8, rows] for back_by in (0, 6, 2, 4)]
         places = [
-            lambda: (gathered.at[tp, rows], z_up),
-            lambda: (gathered.at[tp, rows], z_down),
-            lambda: (gathered.at[tp, rows], sibling),
-            (lambda: (gathered.at[tp, rows], z_far)) if A_DIRECT
-            else (lambda: (gathered.at[(tp + 6) % 8, first], z_up)),
-            lambda: (gathered.at[(tp + 2) % 8, second], z_down),
-            lambda: (gathered.at[(tp + 6) % 8, rows], sibling),
-            lambda: (gathered.at[(tp + 2) % 8, rows], sibling),
-            lambda: (gathered.at[(tp + 4) % 8, rows], sibling),
-            lambda: (kv.at[:, c, y, x, z_lo], z_pair),
-            lambda: (kv.at[0, c, y, x], x_up),
-            lambda: (kv.at[0, c, y, x], x_down),
-            (lambda: (kv.at[0, c, y, x], x_far)) if P1_DIRECT
-            else (lambda: (kv.at[0, c, y, x_lo, 0], x_up)),
-            lambda: (kv.at[0, c, y, x_hi, 1], x_down),
-            lambda: (kv.at[0, c, y], y_up),
-            lambda: (kv.at[0, c, y], y_down),
-            (lambda: (kv.at[0, c, y], y_far)) if P2_DIRECT
-            else (lambda: (kv.at[0, c, y_lo, pl.ds(0, 2)], y_up)),
-            lambda: (kv.at[0, c, y_hi, pl.ds(2, 2)], y_down),
-            lambda: (kv.at[1, c, y, x], y_up),
-            lambda: (kv.at[1, c, y, x], y_down),
-            (lambda: (kv.at[1, c, y, x], y_far)) if P1_DIRECT
-            else (lambda: (kv.at[1, c, y_lo, x, 0], y_up)),
-            lambda: (kv.at[1, c, y_hi, x, 1], y_down),
-            lambda: (kv.at[1, c, :, x], x_up),
-            lambda: (kv.at[1, c, :, x], x_down),
-            (lambda: (kv.at[1, c, :, x], x_far)) if P2_DIRECT
-            else (lambda: (kv.at[1, c, pl.ds(0, 2), x_lo], x_up)),
-            lambda: (kv.at[1, c, pl.ds(2, 2), x_hi], x_down),
+            (tokens[0], z_up), (tokens[0], z_down), (tokens[0], z_far), (tokens[0], sibling),
+            (tokens[1], sibling), (tokens[2], sibling), (tokens[3], sibling),
         ]
-        if number < 25:
-            place, target = places[number]()
+        for other in (x_up, x_down, x_far):
+            places.append((kv.at[0, c, y, x], other))
+        for other in (y_up, y_down, y_far):
+            places.append((kv.at[1, c, y, x], other))
+        for other in (y_up, y_down, y_far):
+            places.append((kv.at[0, c, y], other))
+        for other in (x_up, x_down, x_far):
+            places.append((kv.at[1, c, :, x], other))
+        if number < 19:
+            place, target = places[number]
             source = place
+        elif number == 19:
+            source, place, target = q_here.at[z_lo, 1, :, rows], q_here.at[z_lo, 1, :, rows], z_pair
         else:
             rest = pl.ds(pl.multiple_of((c - NC // 2) * R, R), R)
-            source, place, target = q_away.at[:, rest], q_here.at[0, :, rest], partner
+            source, place = q_away.at[:, rest], q_here.at[z_lo, 0, :, rest]
+            target = partner if number == 20 else diagonal_peer
         return pltpu.make_async_remote_copy(
             src_ref=source, dst_ref=place, send_sem=c_send.at[c, number], recv_sem=c_recv.at[c, number],
             device_id=target, device_id_type=MESH,
@@ -146,8 +127,8 @@
                 normed, wqkv[piece * 512:(piece + 1) * 512, :], preferred_element_type=jnp.float32
             )
         cos_rows, sin_rows = cosine[rows], sine[rows]
-        kv[0, c, y, x, z_lo] = rotate(total[:, 512:640], cos_rows, sin_rows).astype(jnp.bfloat16)
-        kv[1, c, y, x, z_lo] = total[:, 640:768].astype(jnp.bfloat16)
+        kv[0, c, y, x] = rotate(total[:, 512:640], cos_rows, sin_rows).astype(jnp.bfloat16)
+        kv[1, c, y, x] = total[:, 640:768].astype(jnp.bfloat16)
         queries = [
             rotate(total[:, h * 128:(h + 1) * 128], cos_rows, sin_rows).astype(jnp.bfloat16) for h in range(4)
         ]
@@ -155,7 +136,7 @@
         @pl.when(c < NC // 2)
         def _():
             for h in range(4):
-                q_here[1, h, rows] = queries[h]
+                q_here[z_lo, 1, h, rows] = queries[h]
 
         @pl.when(c >= NC // 2)
         def _():
@@ -171,15 +152,15 @@
     def fold(c, half, group, masked):
         keys = kv[0, c, group].reshape(CHUNK_KEYS, HEAD_DIM)
         values = kv[1, c, group].reshape(CHUNK_KEYS, HEAD_DIM)
-        queries = q_here[half].reshape(4 * HALF, HEAD_DIM)
+        queries = q_here[:, half].reshape(8 * HALF, HEAD_DIM)
         scores = lax.dot_general(
             queries, keys, (((1,), (1,)), ((), ())), preferred_element_type=jnp.float32
         )
         if masked:
-            row = lax.broadcasted_iota(jnp.int32, (4 * HALF, 1), 0) % HALF + (1 - half) * HALF
+            index = lax.broadcasted_iota(jnp.int32, (8 * HALF, 1), 0)
+            row = (index // (4 * HALF) * 4 + x) * ROWS + index % HALF + (1 - half) * HALF
             column = lax.broadcasted_iota(jnp.int32, (1, CHUNK_KEYS), 1)
-            block = (column // R) % 2 * 4 + column // (2 * R)
-            key_row = (block - (z_lo * 4 + x)) * ROWS + c * R + column % R
+            key_row = (z_lo * 4 + column // R) * ROWS + c * R + column % R
             scores = jnp.where(key_row <= row, scores, -2e30)
         old = top[half]
         newest = jnp.maximum(old, jnp.max(scores, axis=1, keepdims=True))
@@ -212,99 +193,86 @@
 
         lax.fori_loop(0, 2, diagonal, 0)
 
-    own = (0, 1, 3, 2) if A_DIRECT else (0, 1, 2)
-    if P2_DIRECT:
-        spread, last = (13, 14, 15, 21, 22, 23), (13, 14, 15, 21, 22, 23)
-    else:
-        spread, last = (13, 14, 21, 22), (15, 16, 23, 24)
-    if P1_DIRECT:
-        near = (9, 10, 11, 17, 18, 19)
-    else:
-        near = (9, 10, 17, 18)
-
     for c in range(AHEAD):
-        start(own, c)
+        start((0, 1, 2, 3), c)
 
     def during(t, lag):
         return (t >= lag) & (t < NC + lag)
 
     def tick(t, carry):
-        if not P2_DIRECT:
-            @pl.when(during(t, LAG_S4))
-            def _():
-                arrive((13, 14), t - LAG_S4)
-                start((15, 16), t - LAG_S4)
-                arrive((21, 22), t - LAG_S4)
-                start((23, 24), t - LAG_S4)
-
         @pl.when(during(t, LAG_S3))
         def _():
-            arrive(near if P1_DIRECT else (11, 12, 19, 20), t - LAG_S3)
-            start(spread, t - LAG_S3)
-
-        if not P1_DIRECT:
-            @pl.when(during(t, LAG_S2))
-            def _():
-                arrive((9, 10), t - LAG_S2)
-                start((11, 12), t - LAG_S2)
-                arrive((17, 18), t - LAG_S2)
-                start((19, 20), t - LAG_S2)
-
-        @pl.when(during(t, LAG_S1))
-        def _():
-            arrive((8,), t - LAG_S1)
-            start(near, t - LAG_S1)
-
-        if not A_DIRECT:
-            @pl.when(during(t, LAG_A3))
-            def _():
-                arrive((3, 4), t - LAG_A3)
-                start((7,), t - LAG_A3)
+            arrive(range(7, 13), t - LAG_S3)
+            start(range(13, 19), t - LAG_S3)
 
         @pl.when(t < NC)
         def _():
-            if A_DIRECT:
-                arrive((0, 1, 3), t)
-                start((5, 6, 7), t)
-            else:
-                arrive((0, 1), t)
-                start((3, 4, 5, 6), t)
-
-        @pl.when(t + AHEAD < NC)
-        def _():
-            start(own, t + AHEAD)
-
-        @pl.when(t == LAG_P)
+            arrive((0, 1, 2), t)
+            start((4, 5, 6), t)
+
+        @pl.when(t == 1)
         def _():
             for copy in weights[:3]:
                 copy.wait()
 
-        @pl.when(during(t, LAG_P))
-        def _():
-            arrive((2, 5, 6, 7), t - LAG_P)
-            project(t - LAG_P)
-            start((8,), t - LAG_P)
-
-        @pl.when((t >= NC // 2 + LAG_P) & (t < NC + LAG_P))
-        def _():
-            start((25,), t - LAG_P)
+        @pl.when(during(t, 1))
+        def _():
+            arrive((3, 4, 5, 6), t - 1)
+            project(t - 1)
+            start(range(7, 13), t - 1)
+
+        @pl.when((t >= 1) & (t < NC // 2 + 1))
+        def _():
+            start((19,), t - 1)
+
+        @pl.when((t >= NC // 2 + 1) & (t < NC + 1))
+        def _():
+            start((20, 21), t - 1)
 
         @pl.when(t == LAG_ATT)
         def _():
+            for c in range(NC // 2):
+                arrive((19,), c)
             for c in range(NC // 2, NC):
-                arrive((25,), c)
+                arrive((20, 21), c)
 
         @pl.when(t >= LAG_ATT)
         def _():
-            arrive(last, t - LAG_ATT)
+            arrive(range(13, 19), t - LAG_ATT)
             attend(t - LAG_ATT)
 
         return carry
 
     lax.fori_loop(0, NC + LAG_ATT, tick, 0)
 
+    def returned(at):
+        source, place = ((part_out.at[at], part_in.at[at]) if at < 2 else (log_out, log_in))
+        return pltpu.make_async_remote_copy(
+            src_ref=source, dst_ref=place, send_sem=o_send.at[at], recv_sem=o_recv.at[at],
+            device_id=z_pair, device_id_type=MESH,
+        )
+
+    def partial(half, side):
+        rows = pl.ds(pl.multiple_of(side * 4 * HALF, 4 * HALF), 4 * HALF)
+        return acc[half, rows], top[half, rows], jnp.sum(denom[half, rows], axis=1, keepdims=True)
+
     for half in range(2):
-        whole = acc[half] / jnp.sum(denom[half], axis=1, keepdims=True)
+        whole, highest, total = partial(half, 1 - z_lo)
+        part_out[half] = (whole / jnp.where(total > 0.0, total, 1.0)).astype(jnp.bfloat16)
+        returned(half).start()
+        log_out[half, 0] = highest.T[0:8]
+        log_out[half, 1] = jnp.broadcast_to(total, (4 * HALF, 128)).T[0:8]
+    returned(2).start()
+    for at in range(3):
+        returned(at).wait()
+    for half in range(2):
+        whole, highest, total = partial(half, z_lo)
+        other_highest = jnp.broadcast_to(log_in[half, 0, 0:1], (128, 4 * HALF)).T
+        other_total = jnp.broadcast_to(log_in[half, 1, 0:1], (128, 4 * HALF)).T
+        common = jnp.maximum(highest, other_highest)
+        mine = jnp.exp2((highest - common) * factor_log)
+        theirs = jnp.exp2((other_highest - common) * factor_log) * other_total
+        whole = (whole * mine + part_in[half].astype(jnp.float32) * theirs) / (total * mine + theirs)
         for h in range(4):
             att[half * HALF:(half + 1) * HALF, h * 128:(h + 1) * 128] = whole[
                 h * HALF:(h + 1) * HALF
@@ -389,16 +357,18 @@
 
     lax.fori_loop(0, ND + LAG_D4, out_tick, 0)
 
-    unused = ((4,) if A_DIRECT else ()) + ((12, 20) if P1_DIRECT else ()) + ((16, 24) if P2_DIRECT else ())
-
     def drain_c(c, carry):
-        for number in range(25):
-            if number not in unused:
-                copy_c(number, c).wait_send()
+        for number in range(19):
+            copy_c(number, c).wait_send()
+        return carry
+
+    def drain_near(c, carry):
+        copy_c(19, c).wait_send()
         return carry
 
     def drain_q(c, carry):
-        copy_c(25, c).wait_send()
+        copy_c(20, c).wait_send()
+        copy_c(21, c).wait_send()
         return carry
 
     def drain_d(u, carry):
@@ -411,6 +381,7 @@
         return carry
 
     lax.fori_loop(0, NC, drain_c, 0)
+    lax.fori_loop(0, NC // 2, drain_near, 0)
     lax.fori_loop(NC // 2, NC, drain_q, 0)
     lax.fori_loop(0, ND, drain_d, 0)
     lax.fori_loop(0, ND // 2, drain_y, 0)
@@ -437,12 +408,12 @@
             pltpu.VMEM((8, ROWS, 512), bf16),
             pltpu.VMEM((WIDTH, 768), bf16),
             pltpu.VMEM((512, WIDTH), bf16),
-            pltpu.VMEM((2, NC, 4, 4, 2, R, HEAD_DIM), bf16),
-            pltpu.VMEM((2, 4, HALF, HEAD_DIM), bf16),
+            pltpu.VMEM((2, NC, 4, 4, R, HEAD_DIM), bf16),
+            pltpu.VMEM((2, 2, 4, HALF, HEAD_DIM), bf16),
             pltpu.VMEM((4, HALF, HEAD_DIM), bf16),
-            pltpu.VMEM((2, 4 * HALF, 128), f32),
-            pltpu.VMEM((2, 4 * HALF, 128), f32),
-            pltpu.VMEM((2, 4 * HALF, HEAD_DIM), f32),
+            pltpu.VMEM((2, 8 * HALF, 128), f32),
+            pltpu.VMEM((2, 8 * HALF, 128), f32),
+            pltpu.VMEM((2, 8 * HALF, HEAD_DIM), f32),
             pltpu.VMEM((ROWS, 512), bf16),
             pltpu.VMEM((ND, 4, CR, 512), bf16),
             pltpu.VMEM((ND, 4, CR, 512), bf16),
@@ -452,11 +423,17 @@
             pltpu.VMEM((2, ND, CR, 512), bf16),
             pltpu.VMEM((2, ND, CR, 512), bf16),
             pltpu.VMEM((HALF, 512), bf16),
+            pltpu.VMEM((2, 4 * HALF, HEAD_DIM), bf16),
+            pltpu.VMEM((2, 4 * HALF, HEAD_DIM), bf16),
+            pltpu.VMEM((2, 2, 8, 4 * HALF), f32),
+            pltpu.VMEM((2, 2, 8, 4 * HALF), f32),
             pltpu.SemaphoreType.DMA((5,)),
             pltpu.SemaphoreType.DMA((NC, NS)),
             pltpu.SemaphoreType.DMA((NC, NS)),
             pltpu.SemaphoreType.DMA((ND, MS)),
             pltpu.SemaphoreType.DMA((ND, MS)),
+            pltpu.SemaphoreType.DMA((3,)),
+            pltpu.SemaphoreType.DMA((3,)),
         ],
         compiler_params=pltpu.CompilerParams(
             collective_id=0, has_side_effects=True, vmem_limit_bytes=62 << 20

time: 97.2 us -> 104 us (1.070); the launches traced: 97.1 us -> 103 us
  Pallas kernels: 94 us -> 99.7 us
    pallas_call x1, Pallas kernels: 94 us -> 99.7 us  [body(): pl.pallas_call(sublayer, out_shape=jax.ShapeDtypeStruct((ROWS, 512), bf16...]
where the time goes in v3:
time: 104 us; the launch traced here: 103 us
  Pallas kernels  99.7 us (96%)
  local copies, waits for them, and re-layouts  1.67 us (2%)
  other arithmetic  1.39 us (1%)
    pallas_call x1, Pallas kernels, body(): pl.pallas_call(sublayer, out_shape=jax.ShapeDtypeStruct((ROWS, 512), bf16...  99.7 us

profile of v3, /device:TPU:1, one launch (start us, length us, event | category | flops | bytes accessed | tf_op | source)
XLA Modules:
  0.0 102.8 jit_solution(8736688349479357713)
XLA Ops:
  0.0 0.5 fusion
  0.6 0.8 pad_maximum_fusion
  1.4 99.7 %shard_map.64 = bf16[256,512]{1,0:T(8,128)(2,1)} custom-call(bf16[256,512]{1,0:T(8,128)(2,1)} %tok.1, bf16[4096]{0:T(1024)(128)(2,1)} %gain.1, f32[256,128]{1,0:T(8,128)} %get-tuple-element.8.cosine, f32[256,128]{1,0:T(8,128)} %get-tuple-element.9.sine, bf16[4096,512]{1,0:T(8,128)(2,1)} %wq.1, bf16[4096,128]{1,0:T(8,128)(2,1)} %wk.1, bf16[4096,128]{1,0:T(8,128)(2,1)} %wv.1, ...), custom_call_target="tpu_custom_call" | custom-call | flops 6000000000 | bytes 12000000 | tf_op jit(solution)/shard_map/pallas_call | solution.py:402
  101.1 1.7 %copy.8 = bf16[256,512]{1,0:T(8,128)(2,1)} copy(bf16[256,512]{1,0:T(8,128)(2,1)} %shard_map.64) | data formatting | bytes 524288
  (2 shorter events, 0.0 us)

commit v4 on v2

--- a/solution.py
+++ b/solution.py
@@ -19,8 +19,8 @@
 CR = ROWS // ND
 MS = 6
 AHEAD = 3
-A_DIRECT, P1_DIRECT, P2_DIRECT = False, False, False
-LAG_A3, LAG_P, LAG_S1, LAG_S2, LAG_S3, LAG_S4, LAG_ATT = 2, 3, 5, 7, 9, 11, 13
+A_DIRECT, P1_DIRECT, P2_DIRECT = False, True, False
+LAG_A3, LAG_P, LAG_S1, LAG_S2, LAG_S3, LAG_S4, LAG_ATT = 2, 3, 5, 6, 7, 9, 11
 LAG_D3, LAG_D4 = 1, 3
 CHUNK_KEYS = 8 * R
 LOG2E = 1.4426950408889634
@@ -49,6 +49,8 @@
     y_up = device_at(x, y + 1, z_hi, z_lo, core)
     y_down = device_at(x, y + 3, z_hi, z_lo, core)
     partner = device_at(x, 3 - y, z_hi, z_lo, core)
+    x_far = device_at(x + 2, y, z_hi, z_lo, core)
+    y_far = device_at(x, y + 2, z_hi, z_lo, core)
 
     weights = [
         pltpu.make_async_copy(wq, wqkv.at[:, pl.ds(0, 512)], w_sem.at[0]),
@@ -62,7 +64,7 @@
         copy.start()
 
     barrier = pltpu.get_barrier_semaphore()
-    peers = (z_up, z_down, sibling, z_pair, x_up, x_down, y_up, y_down)
+    peers = (z_up, z_down, sibling, z_pair, x_up, x_down, y_up, y_down, x_far, y_far)
     for peer in peers:
         pl.semaphore_signal(barrier, inc=1, device_id=peer, device_id_type=MESH)
     own_tokens.wait()
@@ -74,8 +76,6 @@
         rows = pl.ds(pl.multiple_of(c * R, R), R)
         first = pl.ds(pl.multiple_of(c * R, R // 2), R // 2)
         second = pl.ds(pl.multiple_of(c * R + R // 2, R // 2), R // 2)
-        x_far = device_at(x + 2, y, z_hi, z_lo, core)
-        y_far = device_at(x, y + 2, z_hi, z_lo, core)
         z_far = device_at(x, y, z_hi + 2, z_lo, core)
         places = [
             lambda: (gathered.at[tp, rows], z_up),

time: 97.2 us -> 95.1 us (0.978); the launches traced: 97.1 us -> 93.6 us
  Pallas kernels: 94 us -> 90.5 us
    pallas_call x1, Pallas kernels: 94 us -> 90.5 us  [body(): pl.pallas_call(sublayer, out_shape=jax.ShapeDtypeStruct((ROWS, 512), bf16...]
where the time goes in v4:
time: 95.1 us; the launch traced here: 93.6 us
  Pallas kernels  90.5 us (95%)
  local copies, waits for them, and re-layouts  1.67 us (2%)
  other arithmetic  1.39 us (1%)
    pallas_call x1, Pallas kernels, body(): pl.pallas_call(sublayer, out_shape=jax.ShapeDtypeStruct((ROWS, 512), bf16...  90.5 us

profile of v4, /device:TPU:1, one launch (start us, length us, event | category | flops | bytes accessed | tf_op | source)
XLA Modules:
  0.0 93.6 jit_solution(4764878015648410410)
XLA Ops:
  0.0 0.5 fusion
  0.6 0.8 pad_maximum_fusion
  1.4 90.5 %shard_map.64 = bf16[256,512]{1,0:T(8,128)(2,1)} custom-call(bf16[256,512]{1,0:T(8,128)(2,1)} %tok.1, bf16[4096]{0:T(1024)(128)(2,1)} %gain.1, f32[256,128]{1,0:T(8,128)} %get-tuple-element.8.cosine, f32[256,128]{1,0:T(8,128)} %get-tuple-element.9.sine, bf16[4096,512]{1,0:T(8,128)(2,1)} %wq.1, bf16[4096,128]{1,0:T(8,128)(2,1)} %wk.1, bf16[4096,128]{1,0:T(8,128)(2,1)} %wv.1, ...), custom_call_target="tpu_custom_call" | custom-call | flops 6000000000 | bytes 12000000 | tf_op jit(solution)/shard_map/pallas_call | solution.py:431
  92.0 1.7 %copy.8 = bf16[256,512]{1,0:T(8,128)(2,1)} copy(bf16[256,512]{1,0:T(8,128)(2,1)} %shard_map.64) | data formatting | bytes 524288
  (2 shorter events, 0.0 us)

commit v5 on v4

--- a/solution.py
+++ b/solution.py
@@ -20,7 +20,7 @@
 MS = 6
 AHEAD = 3
 A_DIRECT, P1_DIRECT, P2_DIRECT = False, True, False
-LAG_A3, LAG_P, LAG_S1, LAG_S2, LAG_S3, LAG_S4, LAG_ATT = 2, 3, 5, 6, 7, 9, 11
+LAG_A3, LAG_P, LAG_S1, LAG_S2, LAG_S3, LAG_S4, LAG_ATT = 2, 3, 4, 5, 6, 8, 10
 LAG_D3, LAG_D4 = 1, 3
 CHUNK_KEYS = 8 * R
 LOG2E = 1.4426950408889634

time: 95.1 us -> 97.2 us (1.022)
  Pallas kernels: 90.5 us -> 93.5 us
    pallas_call x1, Pallas kernels: 90.5 us -> 93.5 us  [body(): pl.pallas_call(sublayer, out_shape=jax.ShapeDtypeStruct((ROWS, 512), bf16...]
where the time goes in v5:
time: 97.2 us; the launch traced here: 96.6 us
  Pallas kernels  93.5 us (96%)
  local copies, waits for them, and re-layouts  1.67 us (2%)
  other arithmetic  1.39 us (1%)
    pallas_call x1, Pallas kernels, body(): pl.pallas_call(sublayer, out_shape=jax.ShapeDtypeStruct((ROWS, 512), bf16...  93.5 us

profile of v5, /device:TPU:1, one launch (start us, length us, event | category | flops | bytes accessed | tf_op | source)
XLA Modules:
  0.0 96.6 jit_solution(6548274670789150148)
XLA Ops:
  0.0 0.5 fusion
  0.6 0.8 pad_maximum_fusion
  1.4 93.5 %shard_map.64 = bf16[256,512]{1,0:T(8,128)(2,1)} custom-call(bf16[256,512]{1,0:T(8,128)(2,1)} %tok.1, bf16[4096]{0:T(1024)(128)(2,1)} %gain.1, f32[256,128]{1,0:T(8,128)} %get-tuple-element.8.cosine, f32[256,128]{1,0:T(8,128)} %get-tuple-element.9.sine, bf16[4096,512]{1,0:T(8,128)(2,1)} %wq.1, bf16[4096,128]{1,0:T(8,128)(2,1)} %wk.1, bf16[4096,128]{1,0:T(8,128)(2,1)} %wv.1, ...), custom_call_target="tpu_custom_call" | custom-call | flops 6000000000 | bytes 12000000 | tf_op jit(solution)/shard_map/pallas_call | solution.py:431
  94.9 1.7 %copy.8 = bf16[256,512]{1,0:T(8,128)(2,1)} copy(bf16[256,512]{1,0:T(8,128)(2,1)} %shard_map.64) | data formatting | bytes 524288
  (2 shorter events, 0.0 us)
